TPU v7x, 512 devices: a whole 4x8x8 slice. The times are simulated.
512 devices in a mesh: sec: 2 (over y_hi), grp: 64 (over y_lo, z, core), tp: 4 (over x).
Axes of the slice: x: 4, y: 8 (y_hi: 2, y_lo: 4; y = y_hi * 4 + y_lo), z: 8, core: 2. Of those that a mesh axis runs over, the one named last changes fastest.
Arguments:
- residual: bfloat16 [256, 6144], P(('sec', 'grp'), 'tp'), may hold values from -30 to 30
- queries: bfloat16 [256, 6144], P(('sec', 'grp'), 'tp'), may hold values from -16 to 16
- key_pages: bfloat16 [3072, 16, 1024], P(('sec', 'grp'), None, 'tp'), may hold values from -32 to 32
- value_pages: bfloat16 [3072, 16, 1024], P(('sec', 'grp'), None, 'tp'), may hold values from -6 to 6
- page_table: int32 [128, 24], P(('sec', 'grp')), may hold values from 0 to 23, each once within a row
- lengths: int32 [128, 2], P(('sec', 'grp')), may hold values from 1 to 192, 288 in all within a row
- norm_gain: bfloat16 [6144], P('tp'), may hold values from 0.099609375 to 1.8984375
- expert_ids: int32 [256, 4], P(('sec', 'grp')), may hold values from 0 to 7, all different within a row; in each aligned block of 2 rows (0 to 1, 2 to 3, ...) at most 2 rows name the same one
- route_gates: float32 [256, 4], P(('sec', 'grp')), may hold values from 0.1 to 1
- w_gate: bfloat16 [6144, 43008], P('tp', ('sec', 'grp')), may hold values from -0.078125 to 0.078125
- w_up: bfloat16 [6144, 43008], P('tp', ('sec', 'grp')), may hold values from -0.078125 to 0.078125
- w_down: bfloat16 [43008, 6144], P(('sec', 'grp'), 'tp'), may hold values from -0.078125 to 0.078125
Outputs:
- layer_out: bfloat16 [256, 6144], P(('sec', 'grp'), 'tp')
Inputs may be any that keep to these rules, and one draw needn't show every extreme that they name: `page_table`: each row lists every local page once; sequence i uses entries i * 12 to i * 12 + 11 in order. The 2 lengths of one row sum to 288; each is at most 192. `expert_ids`: each row names 4 different experts; in each aligned block of 2 rows (the rows of one device) no expert is named by more than 2 rows, and some block names some expert exactly 2 times.
All inputs are finite; a program needn't handle non-finite values.
Results may differ from a plain program's by a relative error of at most 0.0053.
Values may be sent and summed in bfloat16 or wider, within the bound.
A program may use at most 64 MiB of HBM per device.

v0:
```python
import jax
import jax.numpy as jnp
from jax import lax
from jax.sharding import PartitionSpec as P

D = 6144
HEADS = 48
KV_HEADS = 8
HEAD_DIM = 128
EXPERTS = 8
CAP = 2


def shards(
    residual,
    queries,
    key_pages,
    value_pages,
    page_table,
    lengths,
    norm_gain,
    expert_ids,
    route_gates,
    w_gate,
    w_up,
    w_down,
):
    seq_count = residual.shape[0]
    feat_width = residual.shape[1]
    kv_local = key_pages.shape[2] // HEAD_DIM
    group_size = HEADS // KV_HEADS
    page_rows = page_table.reshape(seq_count, -1)
    key_span = page_rows.shape[1] * key_pages.shape[1]
    key_rows = key_pages[page_rows].reshape(seq_count, key_span, kv_local, HEAD_DIM)
    value_rows = value_pages[page_rows].reshape(seq_count, key_span, kv_local, HEAD_DIM)
    query_heads = queries.reshape(seq_count, kv_local, group_size, HEAD_DIM)
    scores = jnp.einsum(
        "sagh,slah->sagl", query_heads, key_rows, preferred_element_type=jnp.float32
    ) * HEAD_DIM ** (-0.5)
    visible = jnp.arange(key_span, dtype=jnp.int32)[None, :] < lengths.reshape(seq_count, 1)
    scores = jnp.where(visible[:, None, None, :], scores, jnp.float32(-1e30))
    top_score = jnp.max(scores, axis=-1, keepdims=True)
    expo = jnp.exp(scores - top_score)
    attn_probs = (expo / jnp.sum(expo, axis=-1, keepdims=True)).astype(jnp.bfloat16)
    attn_out = jnp.einsum(
        "sagl,slah->sagh", attn_probs, value_rows, preferred_element_type=jnp.float32
    )
    attn_out = attn_out.reshape(seq_count, feat_width)
    stream = (residual.astype(jnp.float32) + attn_out).astype(jnp.bfloat16)
    stream_f32 = stream.astype(jnp.float32)
    square_sum = lax.psum(jnp.sum(stream_f32 * stream_f32, axis=1), "tp")
    normed = (
        stream_f32 * lax.rsqrt(square_sum / D + 1e-05)[:, None] * norm_gain.astype(jnp.float32)
    ).astype(jnp.bfloat16)
    route_weight = route_gates / jnp.sum(route_gates, axis=1, keepdims=True)
    matches = expert_ids[:, :, None] == jnp.arange(EXPERTS, dtype=jnp.int32)[None, None, :]
    assign = jnp.sum(matches.astype(jnp.int32), axis=1)
    expert_weight = jnp.sum(matches.astype(jnp.float32) * route_weight[:, :, None], axis=1)
    device_count = lax.axis_size("sec") * lax.axis_size("grp")
    per_expert = device_count // EXPERTS
    slot_rank = jnp.cumsum(assign, axis=0) - assign
    slot_hits = (assign.T[:, None, :] == 1) & (
        slot_rank.T[:, None, :] == jnp.arange(CAP, dtype=jnp.int32)[None, :, None]
    )
    slot_table = slot_hits.astype(jnp.bfloat16)
    packed = jnp.einsum(
        "ecr,rd->ecd", slot_table, normed, preferred_element_type=jnp.float32
    ).astype(jnp.bfloat16)
    combine_table = slot_hits.astype(jnp.float32) * expert_weight.T[:, None, :]
    outbound = jnp.repeat(packed, per_expert, axis=0)
    arrived_rows = lax.all_to_all(outbound, ("sec", "grp"), split_axis=0, concat_axis=0, tiled=True)
    shape_lead = arrived_rows.shape
    row_block = arrived_rows.reshape(-1, feat_width)
    gate_proj = jnp.dot(row_block, w_gate, preferred_element_type=jnp.float32)
    up_proj = jnp.dot(row_block, w_up, preferred_element_type=jnp.float32)
    gate_proj, up_proj = lax.psum((gate_proj, up_proj), "tp")
    hidden = (jax.nn.silu(gate_proj) * up_proj).astype(jnp.bfloat16)
    partial_value = jnp.dot(hidden, w_down, preferred_element_type=jnp.float32).reshape(
        shape_lead[0], shape_lead[1], feat_width
    )
    returned = lax.all_to_all(
        partial_value, ("sec", "grp"), split_axis=0, concat_axis=0, tiled=True
    )
    gathered = jnp.sum(returned.reshape(EXPERTS, per_expert, shape_lead[1], feat_width), axis=1)
    mixture = jnp.einsum("ecr,ecd->rd", combine_table, gathered, precision=lax.Precision.HIGHEST)
    return (stream_f32 + mixture).astype(jnp.bfloat16)


def solution(mesh):
    return jax.shard_map(
        shards,
        mesh=mesh,
        in_specs=(
            P(("sec", "grp"), "tp"),
            P(("sec", "grp"), "tp"),
            P(("sec", "grp"), None, "tp"),
            P(("sec", "grp"), None, "tp"),
            P(("sec", "grp"), None),
            P(("sec", "grp"), None),
            P("tp"),
            P(("sec", "grp"), None),
            P(("sec", "grp"), None),
            P("tp", ("sec", "grp")),
            P("tp", ("sec", "grp")),
            P(("sec", "grp"), "tp"),
        ),
        out_specs=P(("sec", "grp"), "tp"),
        check_vma=False,
    )
```

profile of v0, /device:TPU:1, one launch (start us, length us, event | category | flops | bytes accessed | tf_op | source)
XLA Modules:
  0.0 186.9 jit_solution(16432642944360610242)
XLA Ops:
  6.5 0.9 convert_reduce_fusion
  7.4 0.5 broadcast.90
  8.0 1.3 reduce.3
  9.5 1.5 gather_fusion
  11.0 0.7 reshape.89
  11.7 0.7 iota_compare_fusion.1
  12.4 0.2 fusion.6
  12.6 0.2 fusion.28
  12.8 1.5 gather_fusion.1
  14.4 0.2 fusion.7
  14.8 9.3 %psum.21 = f32[2]{0:T(128)S(1)} all-reduce(f32[2]{0:T(128)S(1)} %get-tuple-element.7), channel_id=1, replica_groups=mesh['sec'=2,'grp'=64,'tp'=4] {'tp'}, use_global_device_ids=true, to_apply=%region_7.8 | all-reduce | flops 2 | bytes 16 | tf_op jit(solution)/shard_map/psum | solution.py:51
  24.1 0.2 convolution_convert_fusion
  24.4 0.4 broadcast_in_dim.16
  24.8 44.5 %all_to_all.10 = bf16[128,2,1536]{2,1,0:T(2,128)(2,1)S(1)} all-to-all(bf16[128,2,1536]{2,1,0:T(2,128)(2,1)S(1)} %bitcast.30), channel_id=1, replica_groups=mesh['sec'=2,'grp'=64,'tp'=4] {'sec','grp'}, dimensions={0} | all-to-all | bytes 1572864 | tf_op jit(solution)/shard_map/all_to_all | solution.py:71
  69.3 0.3 reshape.93
  69.6 2.5 %fusion.29 = f32[256,336]{0,1:T(8,128)} fusion(bf16[256,1536]{1,0:T(8,128)(2,1)S(1)} %reshape.93, bf16[1536,336]{0,1:T(8,128)(2,1)} %param.21), kind=kOutput, calls=%fused_computation.50 | convolution fusion | flops 264241152 | bytes 2162688 | tf_op jit(solution)/shard_map/dot_general | solution.py:74
  72.2 1.2 fusion.30
  73.4 44.4 %all-reduce.3.cloned.1.call-done = (f32[256,336]{0,1:T(8,128)}, f32[256,336]{0,1:T(8,128)}) async-done(((f32[256,336]{0,1:T(8,128)}, f32[256,336]{0,1:T(8,128)}), (f32[256,336]{0,1:T(8,128)}, f32[256,336]{0,1:T(8,128)})) %all-reduce.3.cloned.1.call-update) | async-done | bytes 688144 | tf_op jit(solution)/shard_map/psum | solution.py:76
  117.8 1.7 fusion.10
  119.5 2.1 %reshape.94 = f32[128,2,1536]{2,1,0:T(2,128)} reshape(f32[256,1536]{1,0:T(8,128)S(1)} %fusion.10) | data formatting | bytes 3145728 | tf_op jit(solution)/shard_map/reshape | solution.py:78
  121.6 16.2 %all-to-all-start.1 = ((f32[128,2,1536]{2,1,0:T(2,128)}), f32[128,2,1536]{2,1,0:T(2,128)S(1)}, u32[]{:S(2)}, u32[]{:S(2)}) async-start(f32[128,2,1536]{2,1,0:T(2,128)} %reshape.94), calls=%async_computation.1 | async-start | bytes 3145728 | tf_op jit(solution)/shard_map/all_to_all | solution.py:81
  138.1 40.8 %all-to-all-done.1 = f32[128,2,1536]{2,1,0:T(2,128)S(1)} async-done(((f32[128,2,1536]{2,1,0:T(2,128)}), f32[128,2,1536]{2,1,0:T(2,128)S(1)}, u32[]{:S(2)}, u32[]{:S(2)}) %all-to-all-start.1) | async-done | bytes 1572896 | tf_op jit(solution)/shard_map/all_to_all | solution.py:81
  178.9 0.3 bitcast_reduce_fusion
  179.2 0.8 fusion.2
  (31 shorter events, 0.9 us)
Async XLA Ops:
  6.5 111.2 %copy-start = (bf16[336,1536]{1,0:T(8,128)(2,1)S(1)}, bf16[336,1536]{1,0:T(8,128)(2,1)}, u32[]{:S(2)}) copy-start(bf16[336,1536]{1,0:T(8,128)(2,1)} %param.23) | copy-start | bytes 3096580
  6.5 8.1 %copy-start.2 = (bf16[2,1536]{1,0:T(2,128)(2,1)S(1)}, bf16[2,1536]{1,0:T(2,128)(2,1)}, u32[]{:S(2)}) copy-start(bf16[2,1536]{1,0:T(2,128)(2,1)} %param.12) | copy-start | bytes 18436
  6.5 17.5 %copy-start.3 = (bf16[1536]{0:T(1024)(128)(2,1)S(1)}, bf16[1536]{0:T(1024)(128)(2,1)}, u32[]{:S(2)}) copy-start(bf16[1536]{0:T(1024)(128)(2,1)} %param.18) | copy-start | bytes 9220
  6.5 111.2 %all-reduce.3.cloned.1.call-start = ((), (), s32[]{:S(2)}) async-start(), calls=%async_computation.2 | async-start | bytes 1376256 | tf_op jit(solution)/shard_map/psum | solution.py:76
  69.6 2.5 %copy-start.1 = (bf16[1536,336]{0,1:T(8,128)(2,1)S(1)}, bf16[1536,336]{0,1:T(8,128)(2,1)}, u32[]{:S(2)}) copy-start(bf16[1536,336]{0,1:T(8,128)(2,1)} %param.22) | copy-start | bytes 3096580
  121.6 16.2 %copy-start.5 = (f32[2,4]{1,0:T(2,128)S(1)}, f32[2,4]{1,0:T(2,128)}, u32[]{:S(2)}) copy-start(f32[2,4]{1,0:T(2,128)} %param.20) | copy-start | bytes 100
  121.6 16.4 %copy-start.4 = (s32[2,4]{1,0:T(2,128)S(1)}, s32[2,4]{1,0:T(2,128)}, u32[]{:S(2)}) copy-start(s32[2,4]{1,0:T(2,128)} %param.19) | copy-start | bytes 100
  121.6 57.3 %all-to-all-start.1 = ((f32[128,2,1536]{2,1,0:T(2,128)}), f32[128,2,1536]{2,1,0:T(2,128)S(1)}, u32[]{:S(2)}, u32[]{:S(2)}) async-start(f32[128,2,1536]{2,1,0:T(2,128)} %reshape.94), calls=%async_computation.1 | async-start | bytes 3145728 | tf_op jit(solution)/shard_map/all_to_all | solution.py:81
Sparse Core Ops, SparseCore 0:
  73.5 44.1 all-reduce.2
where the time goes:
time: 187 us
  waiting for transfers between devices  85.2 us (46%)
  blocking collectives  53.8 us (29%)
  starting transfers between devices  16.2 us (9%)
  between operations  13.5 us (7%)
  local copies, waits for them, and re-layouts  7.34 us (4%)
  matrix products  6.92 us (4%)
  other arithmetic  3.89 us (2%)
    all_to_all x1, blocking collectives, shards(): lax.all_to_all(outbound, ('sec', 'grp'), split_axis=0, concat_axis=0, til...  44.5 us
    psum x1, waiting for transfers between devices, shards(): gate_proj, up_proj = lax.psum((gate_proj, up_proj), 'tp')  44.4 us
    all_to_all x1, waiting for transfers between devices, shards(): lax.all_to_all(partial_value, ('sec', 'grp'), split_axis=0, concat_axis=0...  40.8 us
    all_to_all x1, starting transfers between devices, shards(): lax.all_to_all(partial_value, ('sec', 'grp'), split_axis=0, concat_axis=0...  16.2 us
    psum x1, blocking collectives, shards(): square_sum = lax.psum(jnp.sum(stream_f32 * stream_f32, axis=1), 'tp')  9.3 us
  transfers between devices with their start and end apart: 2, of which 2 were waited for; matrix products, arithmetic and copies ran while one was open for 0% of the time, Pallas kernels for 0%

commit v1 on v0

v1 whole, which is shorter than its diff:
```python
import functools

import jax
import jax.numpy as jnp
from jax import lax
from jax.experimental import pallas as pl
from jax.experimental.pallas import tpu as pltpu
from jax.sharding import PartitionSpec as P

MESH = pl.DeviceIdType.MESH
BF16, F32 = jnp.bfloat16, jnp.float32

D = 6144
RING = 8
NX = 4
HEADS_DEV = 12
HD = 128
COLS = 1536
EXT = COLS + HD
FFD = 336
FFP = 384
PAGES = 24
PAGE = 16
KV = PAGES * PAGE
BLK = 32
SS_HI, SS_LO = FFD % HD, FFD % HD + 1

CHUNKS = ((0, 1), (7, 2), (6, 3), (5, 4))
NC = len(CHUNKS)
PLACE = {m: (j, i) for j, pair in enumerate(CHUNKS) for i, m in enumerate(pair)}


def kernel(
    res_hbm, q_hbm, k_hbm, v_hbm, gain_hbm, wg_hbm, wu_hbm, wd_hbm,
    pt, lens, ids, gates,
    out_ref,
    res, q, kp, vp, gain, wg, wu, wd,
    s24, blk, p1, f16, xall, pay, rsb, hid, csend, crecv, r1s, r1r, r2s, r2r,
    ld_sem, p1_s, p1_r, p2_s, p2_r, fw_s, fw_r, rs_s, rs_r, ag_s, ag_r,
    co_s, co_r, r1_s, r1_r, r2_sm, r2_rm,
):
    sec, grp, x = lax.axis_index("sec"), lax.axis_index("grp"), lax.axis_index("tp")
    y, z, c = sec * 4 + grp // 16, (grp // 2) % 8, grp % 2

    def dev(yy, zz, cc, xx):
        return (yy // 4, (yy % 4) * 16 + zz * 2 + cc, xx)

    def first(k):
        return dev((y + k * (1 - c)) % RING, (z + k * c) % RING, c, x)

    def second(k):
        return dev((y + k * c) % RING, (z + k * (1 - c)) % RING, c, x)

    def along(e):
        return dev(y, z, c, (x + e) % NX)

    other = dev(y, z, 1 - c, x)

    loads = []
    for i, (a, b) in enumerate((
        (q_hbm, q), (k_hbm, kp), (v_hbm, vp), (res_hbm, res), (gain_hbm, gain),
        (wg_hbm, wg), (wu_hbm, wu), (wd_hbm, wd.at[pl.ds(0, FFD)]),
    )):
        cp = pltpu.make_async_copy(a, b, ld_sem.at[i])
        cp.start()
        loads.append(cp)

    barrier = pltpu.get_barrier_semaphore()
    peers = [first(k) for k in range(1, RING)] + [second(k) for k in range(1, RING)]
    peers += [along(e) for e in range(1, NX)] + [other]
    for peer in peers:
        pl.semaphore_signal(barrier, inc=1, device_id=peer, device_id_type=MESH)

    pending = []

    def send(src, dst, ssem, rsem, to):
        cp = pltpu.make_async_remote_copy(
            src_ref=src, dst_ref=dst, send_sem=ssem, recv_sem=rsem,
            device_id=to, device_id_type=MESH,
        )
        cp.start()
        pending.append(cp)
        return cp

    lane = lax.broadcasted_iota(jnp.int32, (24, KV), 1)
    row = lax.broadcasted_iota(jnp.int32, (24, KV), 0)
    page = lane // PAGE
    slot = jnp.zeros((24, KV), jnp.int32)
    for j in range(PAGES):
        slot = jnp.where(page == pt[0, j], j, slot)
    late = slot >= PAGES // 2
    pos = (slot - jnp.where(late, PAGES // 2, 0)) * PAGE + lane % PAGE
    visible = (pos < jnp.where(late, lens[0, 1], lens[0, 0])) & (
        jnp.where(late, 1, 0) == row % 2
    )
    lane8 = lax.broadcasted_iota(jnp.int32, (8, HD), 1)
    row8 = lax.broadcasted_iota(jnp.int32, (8, HD), 0)
    weight = jnp.zeros((8, HD), F32)
    total = jnp.ones((8, HD), F32)
    for s in range(2):
        here = row8 == s
        total = jnp.where(
            here, gates[s, 0] + gates[s, 1] + gates[s, 2] + gates[s, 3], total
        )
        for k in range(4):
            hit = here & (lane8 < 16) & (lane8 % 8 == ids[s, k])
            weight = jnp.where(hit, gates[s, k], weight)
    weight = weight / total

    wd[FFD:, :] = jnp.zeros((FFP - FFD, COLS), BF16)

    def stack(value):
        for h in range(HEADS_DEV):
            s24[2 * h : 2 * h + 2, :] = value[:, h * HD : (h + 1) * HD]
        return s24[...]

    nt = (((1,), (1,)), ((), ()))
    loads[0].wait()
    q24 = stack(q[...].astype(F32)).astype(BF16)
    loads[1].wait()
    keys = kp[...].reshape(KV, 2 * HD)
    head0 = row < 12
    scores = jnp.where(
        head0,
        lax.dot_general(q24, keys[:, :HD], nt, preferred_element_type=F32),
        lax.dot_general(q24, keys[:, HD:], nt, preferred_element_type=F32),
    ) * (HD ** -0.5)
    scores = jnp.where(visible, scores, F32(-1e30))
    expo = jnp.exp(scores - jnp.max(scores, axis=1, keepdims=True))
    probs = (expo / jnp.sum(expo, axis=1, keepdims=True)).astype(BF16)
    loads[2].wait()
    values = vp[...].reshape(KV, 2 * HD)
    attn = jnp.dot(probs, values, preferred_element_type=F32)
    row24 = lax.broadcasted_iota(jnp.int32, (24, HD), 0)
    attn = jnp.where(row24 < 12, attn[:, :HD], attn[:, HD:])
    loads[3].wait()
    stream = (stack(res[...].astype(F32)) + attn).astype(BF16).astype(F32)
    loads[4].wait()
    gain24 = stack(jnp.broadcast_to(gain[...].astype(F32), (2, COLS)))
    square = jnp.sum(stream * stream, axis=1, keepdims=True)
    odd = lax.broadcasted_iota(jnp.int32, (24, 1), 0) % 2 == 1
    ss0 = jnp.sum(jnp.where(odd, 0.0, square), axis=0, keepdims=True)
    ss1 = jnp.sum(jnp.where(odd, square, 0.0), axis=0, keepdims=True)
    ss = jnp.where(row8 == 0, ss0, ss1)
    w_hi = weight.astype(BF16).astype(F32)
    ss_hi = ss.astype(BF16).astype(F32)
    extra = jnp.where(lane8 < 8, w_hi, jnp.where(lane8 < 16, weight - w_hi, 0.0))
    extra = jnp.where(lane8 == SS_HI, ss_hi, extra)
    extra = jnp.where(lane8 == SS_LO, ss - ss_hi, extra)
    extra = jnp.where(row8 < 2, extra, 0.0)
    blk[...] = jnp.concatenate([stream * gain24, extra], axis=0).astype(BF16)

    pl.semaphore_wait(barrier, len(peers))

    arrive1 = [
        send(blk, p1.at[k], p1_s.at[k], p1_r.at[k], first(k)) for k in range(1, RING)
    ]

    def place(k, value):
        for t in range(EXT // HD):
            f16[2 * k : 2 * k + 2, t * HD : (t + 1) * HD] = value[2 * t : 2 * t + 2, :]

    place(0, blk[...].astype(F32))
    for k in (1, 7, 2, 6, 3, 5, 4):
        arrive1[k - 1].wait_recv()
        place(k, p1[k].astype(F32))
    xall[0, 0:16, :] = f16[...].astype(BF16)

    arrive2 = [None] * RING
    for m in (4, 5, 3, 6, 2, 7, 1):
        j, i = PLACE[m]
        arrive2[m] = send(
            xall.at[0, pl.ds(0, 16)], xall.at[j, pl.ds(16 * i, 16)],
            p2_s.at[m], p2_r.at[m], second(m),
        )
    loads[5].wait()
    loads[6].wait()
    loads[7].wait()

    rs, ag, core, back = {}, {}, {}, {}

    def gate_up(j):
        for m in CHUNKS[j]:
            if m:
                arrive2[m].wait_recv()
        fw = send(
            xall.at[j, pl.ds(0, 32)], xall.at[j, pl.ds(32, 32)],
            fw_s.at[j], fw_r.at[j], other,
        )
        fw.wait_recv()
        rows = xall[j, :, 0:COLS]
        pay[j, :, :, 256:FFP] = xall[j, :, COLS:EXT].reshape(NX, 16, HD)
        pay[j, :, :, 640:768] = jnp.zeros((NX, 16, HD), BF16)
        pay[j, :, :, 0:FFD] = (
            jnp.dot(rows, wg[...], preferred_element_type=F32).astype(BF16).reshape(NX, 16, FFD)
        )
        pay[j, :, :, FFP : FFP + FFD] = (
            jnp.dot(rows, wu[...], preferred_element_type=F32).astype(BF16).reshape(NX, 16, FFD)
        )
        rs[j] = [
            send(
                pay.at[j, (x + e) % NX], rsb.at[j, e],
                rs_s.at[j, e], rs_r.at[j, e], along(e),
            )
            for e in range(1, NX)
        ]

    lane16 = lax.broadcasted_iota(jnp.int32, (16, FFP), 1)
    tile16 = lax.broadcasted_iota(jnp.int32, (16, HD), 1)

    def activate(j):
        both = pay[j, x].astype(F32)
        for e in range(1, NX):
            rs[j][e - 1].wait_recv()
            both = both + rsb[j, e].astype(F32)
        tile = both[:, 256:FFP]
        square = jnp.sum(
            jnp.where((tile16 == SS_HI) | (tile16 == SS_LO), tile, 0.0),
            axis=1, keepdims=True,
        )
        scale = lax.rsqrt(square / D + 1e-05)
        gate = both[:, 0:FFP] * scale
        up = both[:, FFP:] * scale
        value = gate / (1.0 + jnp.exp(-gate)) * up
        hid[j, x] = jnp.where(lane16 < FFD, value, 0.0).astype(BF16)
        ag[j] = [
            send(hid.at[j, x], hid.at[j, x], ag_s.at[j, e], ag_r.at[j, e], along(e))
            for e in range(1, NX)
        ]

    lane64 = lax.broadcasted_iota(jnp.int32, (64, HD), 1)

    def down(j):
        for e in range(1, NX):
            ag[j][e - 1].wait_recv()
        extras = xall[j, :, COLS:EXT].astype(F32)
        weight = jnp.sum(
            jnp.where((lane64 == y) | (lane64 == y + 8), extras, 0.0),
            axis=1, keepdims=True,
        )
        part = jnp.dot(
            hid[j].reshape(64, FFP), wd[...], preferred_element_type=F32
        ) * weight
        csend[j] = part[32:, :].astype(BF16)
        core[j] = send(csend.at[j], crecv.at[j], co_s.at[j], co_r.at[j], other)
        r1s[j] = part[:32, :].astype(BF16)

    def give_back(j):
        core[j].wait_recv()
        r1s[j] = (r1s[j].astype(F32) + crecv[j].astype(F32)).astype(BF16)
        for i, m in enumerate(CHUNKS[j]):
            if m:
                back[m] = send(
                    r1s.at[j, pl.ds(16 * i, 16)], r1r.at[m],
                    r1_s.at[m], r1_r.at[m], second(RING - m),
                )

    for step in range(NC + 3):
        if step < NC:
            gate_up(step)
        if 0 <= step - 1 < NC:
            activate(step - 1)
        if 0 <= step - 2 < NC:
            down(step - 2)
        if 0 <= step - 3 < NC:
            give_back(step - 3)

    f16[:, 0:COLS] = r1s[0, 0:16, :].astype(F32)
    for m in (1, 7, 2, 6, 3, 5, 4):
        back[m].wait_recv()
        f16[:, 0:COLS] += r1r[m].astype(F32)

    home = []
    for k in range(RING):
        for h in range(HEADS_DEV):
            s24[2 * h : 2 * h + 2, :] = f16[2 * k : 2 * k + 2, h * HD : (h + 1) * HD]
        if k == 0:
            mixture = s24[...]
        else:
            r2s[k, 0:24, :] = s24[...].astype(BF16)
            r2s[k, 24:32, :] = jnp.zeros((8, HD), BF16)
            home.append(
                send(r2s.at[k], r2r.at[k], r2_sm.at[k], r2_rm.at[k], first(RING - k))
            )
    for k in (1, 7, 2, 6, 3, 5, 4):
        home[k - 1].wait_recv()
        mixture = mixture + r2r[k, 0:24, :].astype(F32)
    out_ref[...] = (stream + mixture).astype(BF16)
    for cp in pending:
        cp.wait_send()


def shards(
    residual, queries, key_pages, value_pages, page_table, lengths, norm_gain,
    expert_ids, route_gates, w_gate, w_up, w_down,
):
    any_, smem = pl.BlockSpec(memory_space=pl.ANY), pl.BlockSpec(memory_space=pltpu.SMEM)
    dma = pltpu.SemaphoreType.DMA
    out = pl.pallas_call(
        kernel,
        out_shape=jax.ShapeDtypeStruct((24, HD), BF16),
        in_specs=[any_] * 8 + [smem] * 4,
        out_specs=pl.BlockSpec(memory_space=pltpu.VMEM),
        scratch_shapes=[
            pltpu.VMEM((2, COLS), BF16), pltpu.VMEM((2, COLS), BF16),
            pltpu.VMEM((PAGES, PAGE, 2 * HD), BF16), pltpu.VMEM((PAGES, PAGE, 2 * HD), BF16),
            pltpu.VMEM((1, COLS), BF16),
            pltpu.VMEM((COLS, FFD), BF16), pltpu.VMEM((COLS, FFD), BF16),
            pltpu.VMEM((FFP, COLS), BF16),
            pltpu.VMEM((24, HD), F32), pltpu.VMEM((BLK, HD), BF16),
            pltpu.VMEM((RING, BLK, HD), BF16), pltpu.VMEM((16, EXT), F32),
            pltpu.VMEM((NC, 64, EXT), BF16), pltpu.VMEM((NC, NX, 16, 2 * FFP), BF16),
            pltpu.VMEM((NC, NX, 16, 2 * FFP), BF16), pltpu.VMEM((NC, NX, 16, FFP), BF16),
            pltpu.VMEM((NC, 32, COLS), BF16), pltpu.VMEM((NC, 32, COLS), BF16),
            pltpu.VMEM((NC, 32, COLS), BF16), pltpu.VMEM((RING, 16, COLS), BF16),
            pltpu.VMEM((RING, BLK, HD), BF16), pltpu.VMEM((RING, BLK, HD), BF16),
            dma((8,)), dma((RING,)), dma((RING,)), dma((RING,)), dma((RING,)),
            dma((NC,)), dma((NC,)), dma((NC, NX)), dma((NC, NX)), dma((NC, NX)), dma((NC, NX)),
            dma((NC,)), dma((NC,)), dma((RING,)), dma((RING,)), dma((RING,)), dma((RING,)),
        ],
        compiler_params=pltpu.CompilerParams(
            collective_id=0, has_side_effects=True, vmem_limit_bytes=48 * 2**20
        ),
        name="decode_layer",
    )(
        residual, queries, key_pages, value_pages, norm_gain.reshape(1, COLS),
        w_gate, w_up, w_down, page_table, lengths, expert_ids, route_gates,
    )
    return out.reshape(HEADS_DEV, 2, HD).transpose(1, 0, 2).reshape(2, COLS)


def solution(mesh):
    rows, wide = ("sec", "grp"), "tp"
    return jax.shard_map(
        shards,
        mesh=mesh,
        in_specs=(
            P(rows, wide), P(rows, wide), P(rows, None, wide), P(rows, None, wide),
            P(rows, None), P(rows, None), P(wide), P(rows, None), P(rows, None),
            P(wide, rows), P(wide, rows), P(rows, wide),
        ),
        out_specs=P(rows, wide),
        check_vma=False,
    )
```

time: 187 us -> 67.2 us (0.36)
  the two profiles are of different devices: /device:TPU:1 before, /device:TPU:8 now
where the time goes in v1:
time: 67.2 us; the launch traced here: 66.9 us
  Pallas kernels  60.2 us (90%)
  local copies, waits for them, and re-layouts  6.61 us (10%)
    pallas_call x1, Pallas kernels, shards(): pl.pallas_call(kernel, out_shape=jax.ShapeDtypeStruct((24, HD), BF16), in...  60.2 us
    unnamed x21, local copies, waits for them, and re-layouts  5.91 us

profile of v1, /device:TPU:8, one launch (start us, length us, event | category | flops | bytes accessed | tf_op | source)
XLA Modules:
  0.0 66.9 jit_solution(3132380575964467369)
XLA Ops:
  0.0 0.7 %reshape.9.gain_hbm = bf16[1,1536]{1,0:T(2,128)(2,1)S(1)} reshape(bf16[1536]{0:T(1024)(128)(2,1)} %param.18) | data formatting | bytes 6144 | tf_op jit(solution)/shard_map/reshape | solution.py:326
  0.7 1.7 %copy.16.wg_hbm = bf16[1536,336]{1,0:T(8,128)(2,1)S(1)} copy(bf16[1536,336]{0,1:T(8,128)(2,1)} %param.21) | data formatting | bytes 2064384 | tf_op args[9]
  2.4 0.0 copy-start
  2.4 0.0 copy-start.3
  2.4 0.0 copy-start.4
  2.4 0.0 copy-start.5
  2.4 0.0 copy-start.6
  2.4 0.0 copy-start.7
  2.4 0.0 copy-start.8
  2.5 1.7 %copy.17.wu_hbm = bf16[1536,336]{1,0:T(8,128)(2,1)S(1)} copy(bf16[1536,336]{0,1:T(8,128)(2,1)} %param.22) | data formatting | bytes 2064384 | tf_op args[10]
  4.2 0.0 copy-done
  4.2 0.0 copy-done.3
  4.2 0.0 copy-done.4
  4.2 0.0 copy-done.5
  4.3 0.0 copy-done.6
  4.3 0.0 copy-done.7
  4.3 0.0 copy-done.8
  4.3 0.0 copy-start.1
  4.3 0.9 %copy-done.1 = bf16[24,16,256]{2,1,0:T(8,128)(2,1)S(1)} copy-done((bf16[24,16,256]{2,1,0:T(8,128)(2,1)S(1)}, bf16[24,16,256]{2,1,0:T(8,128)(2,1)}, u32[]{:S(2)}) %copy-start.1) | copy-done | bytes 196632
  5.2 0.0 copy-start.2
  5.2 0.9 %copy-done.2 = bf16[24,16,256]{2,1,0:T(8,128)(2,1)S(1)} copy-done((bf16[24,16,256]{2,1,0:T(8,128)(2,1)S(1)}, bf16[24,16,256]{2,1,0:T(8,128)(2,1)}, u32[]{:S(2)}) %copy-start.2) | copy-done | bytes 196632
  6.1 60.2 %decode_layer.1 = bf16[24,128]{1,0:T(8,128)(2,1)S(1)} custom-call(bf16[2,1536]{1,0:T(2,128)(2,1)S(1)} %copy-done.3, bf16[2,1536]{1,0:T(2,128)(2,1)S(1)} %copy-done.4, bf16[24,16,256]{2,1,0:T(8,128)(2,1)S(1)} %copy-done.1, bf16[24,16,256]{2,1,0:T(8,128)(2,1)S(1)} %copy-done.2, bf16[1,1536]{1,0:T(2,128)(2,1)S(1)} %reshape.9.gain_hbm, ...), custom_call_target="tpu_custom_call" | custom-call | tf_op jit(solution)/shard_map/decode_layer/pallas_call | solution.py:299
  66.3 0.6 copy.23
  (1 shorter events, 0.0 us)
Async XLA Ops:
  2.4 1.8 %copy-start = (bf16[336,1536]{1,0:T(8,128)(2,1)S(1)}, bf16[336,1536]{1,0:T(8,128)(2,1)}, u32[]{:S(2)}) copy-start(bf16[336,1536]{1,0:T(8,128)(2,1)} %wd_hbm.1) | copy-start | bytes 3096580
  2.4 1.8 %copy-start.3 = (bf16[2,1536]{1,0:T(2,128)(2,1)S(1)}, bf16[2,1536]{1,0:T(2,128)(2,1)}, u32[]{:S(2)}) copy-start(bf16[2,1536]{1,0:T(2,128)(2,1)} %res_hbm.1) | copy-start | bytes 18436
  2.4 1.8 %copy-start.4 = (bf16[2,1536]{1,0:T(2,128)(2,1)S(1)}, bf16[2,1536]{1,0:T(2,128)(2,1)}, u32[]{:S(2)}) copy-start(bf16[2,1536]{1,0:T(2,128)(2,1)} %q_hbm.1) | copy-start | bytes 18436
  2.4 1.8 %copy-start.5 = (s32[2,4]{1,0:T(2,128)S(1)}, s32[2,4]{1,0:T(2,128)}, u32[]{:S(2)}) copy-start(s32[2,4]{1,0:T(2,128)} %ids.1) | copy-start | bytes 100
  2.4 1.8 %copy-start.6 = (f32[2,4]{1,0:T(2,128)S(1)}, f32[2,4]{1,0:T(2,128)}, u32[]{:S(2)}) copy-start(f32[2,4]{1,0:T(2,128)} %gates.1) | copy-start | bytes 100
  2.4 1.8 %copy-start.7 = (s32[1,24]{1,0:T(1,128)S(1)}, s32[1,24]{1,0:T(1,128)}, u32[]{:S(2)}) copy-start(s32[1,24]{1,0:T(1,128)} %pt.1) | copy-start | bytes 292
  2.4 1.8 %copy-start.8 = (s32[1,2]{1,0:T(1,128)S(1)}, s32[1,2]{1,0:T(1,128)}, u32[]{:S(2)}) copy-start(s32[1,2]{1,0:T(1,128)} %lens.1) | copy-start | bytes 28
  4.3 0.9 %copy-start.1 = (bf16[24,16,256]{2,1,0:T(8,128)(2,1)S(1)}, bf16[24,16,256]{2,1,0:T(8,128)(2,1)}, u32[]{:S(2)}) copy-start(bf16[24,16,256]{2,1,0:T(8,128)(2,1)} %k_hbm.1) | copy-start | bytes 589828
  5.2 0.9 %copy-start.2 = (bf16[24,16,256]{2,1,0:T(8,128)(2,1)S(1)}, bf16[24,16,256]{2,1,0:T(8,128)(2,1)}, u32[]{:S(2)}) copy-start(bf16[24,16,256]{2,1,0:T(8,128)(2,1)} %v_hbm.1) | copy-start | bytes 589828

commit v2 on v1

v2 whole, which is shorter than its diff:
```python
import functools

import jax
import jax.numpy as jnp
from jax import lax
from jax.experimental import pallas as pl
from jax.experimental.pallas import tpu as pltpu
from jax.sharding import PartitionSpec as P

MESH = pl.DeviceIdType.MESH
BF16, F32 = jnp.bfloat16, jnp.float32

D = 6144
RING = 8
NX = 4
HEADS_DEV = 12
HD = 128
COLS = 1536
EXT = COLS + HD
FFD = 336
FFP = 384
PAGES = 24
PAGE = 16
KV = PAGES * PAGE
BLK = 32
SS_HI, SS_LO = FFD % HD, FFD % HD + 1

CHUNKS = ((4, 5, 3, 6), (7, 2, 1, 0))
STEPS = "F0 G0 F1 G1 A0 A1 D0 E0 D1 E1"
NC = len(CHUNKS)
BASE = [sum(len(c) for c in CHUNKS[:j]) for j in range(NC)]
ROW = {m: 32 * BASE[j] + 16 * i for j, c in enumerate(CHUNKS) for i, m in enumerate(c)}
HALF = {m: 16 * (BASE[j] + i) for j, c in enumerate(CHUNKS) for i, m in enumerate(c)}
FAR = (4, 5, 3, 6, 2, 7, 1)
NEAR = FAR[::-1]


def kernel(
    res_hbm, q_hbm, k_hbm, v_hbm, gain_hbm, wg_hbm, wu_hbm, wd_hbm,
    pt_hbm, lens_hbm, ids_hbm, gates_hbm,
    out_ref,
    pt, lens, ids, gates, res, q, kp, vp, gain, wgu, wd,
    s24, blk, p1, f16, xall, pay, rsb, hid, csend, crecv, r1s, r1r, r2s, r2r,
    ld_sem, p1_s, p1_r, p2_s, p2_r, fw_s, fw_r, rs_s, rs_r, ag_s, ag_r,
    co_s, co_r, r1_s, r1_r, r2_sm, r2_rm,
):
    sec, grp, x = lax.axis_index("sec"), lax.axis_index("grp"), lax.axis_index("tp")
    y, z, c = sec * 4 + grp // 16, (grp // 2) % 8, grp % 2

    def dev(yy, zz, cc, xx):
        return (yy // 4, (yy % 4) * 16 + zz * 2 + cc, xx)

    def first(k):
        return dev((y + k * (1 - c)) % RING, (z + k * c) % RING, c, x)

    def second(k):
        return dev((y + k * c) % RING, (z + k * (1 - c)) % RING, c, x)

    def along(e):
        return dev(y, z, c, (x + e) % NX)

    other = dev(y, z, 1 - c, x)

    barrier = pltpu.get_barrier_semaphore()
    peers = [ring(k) for k in FAR for ring in (first, second)]
    peers += [along(e) for e in range(1, NX)] + [other]
    for peer in peers:
        pl.semaphore_signal(barrier, inc=1, device_id=peer, device_id_type=MESH)

    loads = []
    for i, (a, b) in enumerate((
        (pt_hbm, pt), (lens_hbm, lens), (ids_hbm, ids), (gates_hbm, gates),
        (q_hbm, q), (k_hbm, kp), (v_hbm, vp), (res_hbm, res), (gain_hbm, gain),
        (wg_hbm, wgu.at[pl.ds(0, FFD)]), (wu_hbm, wgu.at[pl.ds(FFP, FFD)]),
        (wd_hbm, wd.at[pl.ds(0, FFD)]),
    )):
        cp = pltpu.make_async_copy(a, b, ld_sem.at[i])
        cp.start()
        loads.append(cp)

    pending = []

    def send(src, dst, ssem, rsem, to):
        cp = pltpu.make_async_remote_copy(
            src_ref=src, dst_ref=dst, send_sem=ssem, recv_sem=rsem,
            device_id=to, device_id_type=MESH,
        )
        cp.start()
        pending.append(cp)
        return cp

    lane = lax.broadcasted_iota(jnp.int32, (8, KV), 1)
    row = lax.broadcasted_iota(jnp.int32, (8, KV), 0)
    page = lane // PAGE
    slot = jnp.zeros((8, KV), jnp.int32)
    loads[0].wait()
    loads[1].wait()
    for j in range(PAGES):
        slot = jnp.where(page == pt[0, j], j, slot)
    late = slot >= PAGES // 2
    pos = (slot - jnp.where(late, PAGES // 2, 0)) * PAGE + lane % PAGE
    visible = (pos < jnp.where(late, lens[0, 1], lens[0, 0])) & (
        jnp.where(late, 1, 0) == row % 2
    )
    hidden_tokens = jnp.where(visible, 0.0, F32(-1e30))
    hidden_tokens = jnp.concatenate([hidden_tokens] * 3, axis=0)
    loads[2].wait()
    loads[3].wait()
    lane8 = lax.broadcasted_iota(jnp.int32, (8, HD), 1)
    row8 = lax.broadcasted_iota(jnp.int32, (8, HD), 0)
    weight = jnp.zeros((8, HD), F32)
    total = jnp.ones((8, HD), F32)
    for s in range(2):
        here = row8 == s
        total = jnp.where(
            here, gates[s, 0] + gates[s, 1] + gates[s, 2] + gates[s, 3], total
        )
        for k in range(4):
            hit = here & (lane8 < 16) & (lane8 % 8 == ids[s, k])
            weight = jnp.where(hit, gates[s, k], weight)
    weight = weight / total

    wd[FFD:, :] = jnp.zeros((FFP - FFD, COLS), BF16)
    wgu[FFD:FFP, :] = jnp.zeros((FFP - FFD, COLS), BF16)
    wgu[FFP + FFD :, :] = jnp.zeros((FFP - FFD, COLS), BF16)

    def stack(value):
        for h in range(HEADS_DEV):
            s24[2 * h : 2 * h + 2, :] = value[:, h * HD : (h + 1) * HD]
        return s24[...]

    nt = (((1,), (1,)), ((), ()))
    loads[4].wait()
    q24 = stack(q[...].astype(F32)).astype(BF16)
    loads[5].wait()
    keys = kp[...].reshape(KV, 2 * HD)
    head0 = lax.broadcasted_iota(jnp.int32, (24, KV), 0) < 12
    scores = jnp.where(
        head0,
        lax.dot_general(q24, keys[:, :HD], nt, preferred_element_type=F32),
        lax.dot_general(q24, keys[:, HD:], nt, preferred_element_type=F32),
    ) * (HD ** -0.5)
    scores = jnp.where(hidden_tokens < 0.0, hidden_tokens, scores)
    expo = jnp.exp(scores - jnp.max(scores, axis=1, keepdims=True))
    probs = (expo / jnp.sum(expo, axis=1, keepdims=True)).astype(BF16)
    loads[6].wait()
    values = vp[...].reshape(KV, 2 * HD)
    attn = jnp.dot(probs, values, preferred_element_type=F32)
    row24 = lax.broadcasted_iota(jnp.int32, (24, HD), 0)
    attn = jnp.where(row24 < 12, attn[:, :HD], attn[:, HD:])
    loads[7].wait()
    stream = (stack(res[...].astype(F32)) + attn).astype(BF16).astype(F32)
    loads[8].wait()
    gains = gain[...].astype(F32).reshape(HEADS_DEV, HD)
    for h in range(HEADS_DEV):
        s24[2 * h : 2 * h + 2, :] = jnp.broadcast_to(gains[h : h + 1, :], (2, HD))
    gain24 = s24[...]
    square = jnp.sum(stream * stream, axis=1, keepdims=True)
    odd = lax.broadcasted_iota(jnp.int32, (24, 1), 0) % 2 == 1
    ss0 = jnp.sum(jnp.where(odd, 0.0, square), axis=0, keepdims=True)
    ss1 = jnp.sum(jnp.where(odd, square, 0.0), axis=0, keepdims=True)
    ss = jnp.where(row8 == 0, ss0, ss1)
    w_hi = weight.astype(BF16).astype(F32)
    ss_hi = ss.astype(BF16).astype(F32)
    extra = jnp.where(lane8 < 8, w_hi, jnp.where(lane8 < 16, weight - w_hi, 0.0))
    extra = jnp.where(lane8 == SS_HI, ss_hi, extra)
    extra = jnp.where(lane8 == SS_LO, ss - ss_hi, extra)
    extra = jnp.where(row8 < 2, extra, 0.0)
    blk[...] = jnp.concatenate([stream * gain24, extra], axis=0).astype(BF16)

    pl.semaphore_wait(barrier, len(peers))

    arrive1 = [
        send(blk, p1.at[k], p1_s.at[k], p1_r.at[k], first(k)) for k in range(1, RING)
    ]

    def place(k, value):
        for t in range(EXT // HD):
            f16[2 * k : 2 * k + 2, t * HD : (t + 1) * HD] = value[2 * t : 2 * t + 2, :]

    place(0, blk[...].astype(F32))
    for k in NEAR:
        arrive1[k - 1].wait_recv()
        place(k, p1[k].astype(F32))
    own = pl.ds(ROW[0], 16)
    xall[own, :] = f16[...].astype(BF16)

    arrive2 = {
        m: send(
            xall.at[own], xall.at[pl.ds(ROW[m], 16)], p2_s.at[m], p2_r.at[m], second(m)
        )
        for m in FAR
    }
    for cp in loads[9:]:
        cp.wait()

    forwards, rs, ag, core, back = {}, {}, {}, {}, {}

    def quarter(j, q):
        size = 8 * len(CHUNKS[j])
        return pl.ds(pl.multiple_of(32 * BASE[j] + q * size, 16), size)

    def forward(j):
        n, base = len(CHUNKS[j]), 32 * BASE[j]
        forwards[j] = []
        for i, m in enumerate(CHUNKS[j]):
            if m:
                arrive2[m].wait_recv()
            forwards[j].append(send(
                xall.at[pl.ds(base + 16 * i, 16)],
                xall.at[pl.ds(base + 16 * (n + i), 16)],
                fw_s.at[m], fw_r.at[m], other,
            ))

    def gate_up(j):
        n, base = len(CHUNKS[j]), 32 * BASE[j]
        for cp in forwards[j]:
            cp.wait_recv()
        rows = pl.ds(base, 32 * n)
        both = lax.dot_general(
            xall[rows, 0:COLS], wgu[...], nt, preferred_element_type=F32
        )
        lane = lax.broadcasted_iota(jnp.int32, (32 * n, HD), 1)
        extras = xall[rows, COLS:EXT].astype(F32)
        tile = jnp.where(lane >= FFD % HD, extras, both[:, 256:FFP])
        pay[rows, 0:256] = both[:, 0:256].astype(BF16)
        pay[rows, 256:FFP] = tile.astype(BF16)
        pay[rows, FFP:] = both[:, FFP:].astype(BF16)
        piece = pl.ds(8 * BASE[j], 8 * n)
        rs[j] = [
            send(
                pay.at[quarter(j, (x + e) % NX)], rsb.at[e, piece],
                rs_s.at[j, e], rs_r.at[j, e], along(e),
            )
            for e in (2, 1, 3)
        ]

    def activate(j):
        n = len(CHUNKS[j])
        both = pay[quarter(j, x), :].astype(F32)
        lane = lax.broadcasted_iota(jnp.int32, (8 * n, HD), 1)
        weight = jnp.sum(
            jnp.where(
                (lane == y) | (lane == y + 8),
                xall[quarter(j, x), COLS:EXT].astype(F32), 0.0,
            ),
            axis=1, keepdims=True,
        )
        for cp, e in zip(rs[j], (2, 1, 3)):
            cp.wait_recv()
            both = both + rsb[e, pl.ds(8 * BASE[j], 8 * n), :].astype(F32)
        square = jnp.sum(
            jnp.where((lane == SS_HI) | (lane == SS_LO), both[:, 256:FFP], 0.0),
            axis=1, keepdims=True,
        )
        scale = lax.rsqrt(square / D + 1e-05)
        gate = both[:, 0:FFP] * scale
        up = both[:, FFP:] * (scale * weight)
        value = gate / (1.0 + jnp.exp(-gate)) * up
        unit = lax.broadcasted_iota(jnp.int32, (8 * n, FFP), 1)
        mine = quarter(j, x)
        hid[mine, :] = jnp.where(unit < FFD, value, 0.0).astype(BF16)
        ag[j] = [
            send(hid.at[mine], hid.at[mine], ag_s.at[j, e], ag_r.at[j, e], along(e))
            for e in (2, 1, 3)
        ]

    def down(j):
        n, base = len(CHUNKS[j]), 32 * BASE[j]
        half = pl.ds(16 * BASE[j], 16 * n)
        for cp in ag[j]:
            cp.wait_recv()
        theirs = pl.ds(base + 16 * n, 16 * n)
        csend[half, :] = jnp.dot(
            hid[theirs, :], wd[...], preferred_element_type=F32
        ).astype(BF16)
        core[j] = send(csend.at[half], crecv.at[half], co_s.at[j], co_r.at[j], other)
        mine = pl.ds(base, 16 * n)
        r1s[half, :] = jnp.dot(
            hid[mine, :], wd[...], preferred_element_type=F32
        ).astype(BF16)

    def give_back(j):
        core[j].wait_recv()
        half = pl.ds(16 * BASE[j], 16 * len(CHUNKS[j]))
        r1s[half, :] = (r1s[half, :].astype(F32) + crecv[half, :].astype(F32)).astype(BF16)
        for m in FAR:
            if m in CHUNKS[j]:
                back[m] = send(
                    r1s.at[pl.ds(HALF[m], 16)], r1r.at[m],
                    r1_s.at[m], r1_r.at[m], second(RING - m),
                )

    stages = {"F": forward, "G": gate_up, "A": activate, "D": down, "E": give_back}
    for step in STEPS.split():
        stages[step[0]](int(step[1:]))

    total = r1s[pl.ds(HALF[0], 16), :].astype(F32)
    for m in NEAR:
        back[m].wait_recv()
        total = total + r1r[m].astype(F32)
    f16[:, 0:COLS] = total

    home = {}
    for k in FAR + (0,):
        for h in range(HEADS_DEV):
            s24[2 * h : 2 * h + 2, :] = f16[2 * k : 2 * k + 2, h * HD : (h + 1) * HD]
        if k:
            r2s[k, 0:24, :] = s24[...].astype(BF16)
            r2s[k, 24:32, :] = jnp.zeros((8, HD), BF16)
            home[k] = send(
                r2s.at[k], r2r.at[k], r2_sm.at[k], r2_rm.at[k], first(RING - k)
            )
    mixture = s24[...]
    for cp in pending[: -len(FAR)]:
        cp.wait_send()
    for k in NEAR:
        home[k].wait_recv()
        mixture = mixture + r2r[k, 0:24, :].astype(F32)
    out_ref[...] = (stream + mixture).astype(BF16)
    for cp in pending[-len(FAR) :]:
        cp.wait_send()


def shards(
    residual, queries, key_pages, value_pages, page_table, lengths, norm_gain,
    expert_ids, route_gates, w_gate, w_up, w_down,
):
    any_ = pl.BlockSpec(memory_space=pl.ANY)
    dma = pltpu.SemaphoreType.DMA
    out = pl.pallas_call(
        kernel,
        out_shape=jax.ShapeDtypeStruct((24, HD), BF16),
        in_specs=[any_] * 12,
        out_specs=pl.BlockSpec(memory_space=pltpu.VMEM),
        scratch_shapes=[
            pltpu.SMEM((1, PAGES), jnp.int32), pltpu.SMEM((1, 2), jnp.int32),
            pltpu.SMEM((2, 4), jnp.int32), pltpu.SMEM((2, 4), F32),
            pltpu.VMEM((2, COLS), BF16), pltpu.VMEM((2, COLS), BF16),
            pltpu.VMEM((PAGES, PAGE, 2 * HD), BF16), pltpu.VMEM((PAGES, PAGE, 2 * HD), BF16),
            pltpu.VMEM((COLS,), BF16),
            pltpu.VMEM((2 * FFP, COLS), BF16),
            pltpu.VMEM((FFP, COLS), BF16),
            pltpu.VMEM((24, HD), F32), pltpu.VMEM((BLK, HD), BF16),
            pltpu.VMEM((RING, BLK, HD), BF16), pltpu.VMEM((16, EXT), F32),
            pltpu.VMEM((256, EXT), BF16), pltpu.VMEM((256, 2 * FFP), BF16),
            pltpu.VMEM((NX, 64, 2 * FFP), BF16), pltpu.VMEM((256, FFP), BF16),
            pltpu.VMEM((128, COLS), BF16), pltpu.VMEM((128, COLS), BF16),
            pltpu.VMEM((128, COLS), BF16), pltpu.VMEM((RING, 16, COLS), BF16),
            pltpu.VMEM((RING, BLK, HD), BF16), pltpu.VMEM((RING, BLK, HD), BF16),
            dma((12,)), dma((RING,)), dma((RING,)), dma((RING,)), dma((RING,)),
            dma((RING,)), dma((RING,)), dma((NC, NX)), dma((NC, NX)), dma((NC, NX)), dma((NC, NX)),
            dma((NC,)), dma((NC,)), dma((RING,)), dma((RING,)), dma((RING,)), dma((RING,)),
        ],
        compiler_params=pltpu.CompilerParams(
            collective_id=0, has_side_effects=True, vmem_limit_bytes=60 * 2**20
        ),
        name="decode_layer",
    )(
        residual, queries, key_pages, value_pages, norm_gain,
        w_gate.T, w_up.T, w_down, page_table, lengths, expert_ids, route_gates,
    )
    return out.reshape(HEADS_DEV, 2, HD).transpose(1, 0, 2).reshape(2, COLS)


def solution(mesh):
    rows, wide = ("sec", "grp"), "tp"
    return jax.shard_map(
        shards,
        mesh=mesh,
        in_specs=(
            P(rows, wide), P(rows, wide), P(rows, None, wide), P(rows, None, wide),
            P(rows, None), P(rows, None), P(wide), P(rows, None), P(rows, None),
            P(wide, rows), P(wide, rows), P(rows, wide),
        ),
        out_specs=P(rows, wide),
        check_vma=False,
    )
```

time: 67.2 us -> 52.4 us (0.78)
  the two profiles are of different devices: /device:TPU:8 before, /device:TPU:1 now
where the time goes in v2:
time: 52.4 us; the launch traced here: 52.2 us
  Pallas kernels  50.9 us (97%)
  local copies, waits for them, and re-layouts  1.3 us (2%)
    pallas_call x1, Pallas kernels, shards(): pl.pallas_call(kernel, out_shape=jax.ShapeDtypeStruct((24, HD), BF16), in...  50.9 us

profile of v2, /device:TPU:1, one launch (start us, length us, event | category | flops | bytes accessed | tf_op | source)
XLA Modules:
  0.0 52.2 jit_solution(15861043506185120347)
XLA Ops:
  0.0 50.9 %decode_layer.1 = bf16[24,128]{1,0:T(8,128)(2,1)} custom-call(bf16[2,1536]{1,0:T(2,128)(2,1)} %res_hbm.1, bf16[2,1536]{1,0:T(2,128)(2,1)} %q_hbm.1, bf16[24,16,256]{2,1,0:T(8,128)(2,1)} %k_hbm.1, bf16[24,16,256]{2,1,0:T(8,128)(2,1)} %v_hbm.1, bf16[1536]{0:T(1024)(128)(2,1)} %gain_hbm.1, bf16[336,1536]{1,0:T(8,128)(2,1)} %bitcast.10, ...), custom_call_target="tpu_custom_call" | custom-call | tf_op jit(solution)/shard_map/decode_layer/pallas_call | solution.py:331
  50.9 0.7 %copy.18 = bf16[12,2,128]{2,0,1:T(8,128)(2,1)S(1)} copy(bf16[12,2,128]{2,1,0:T(2,128)(2,1)} %bitcast.13) | data formatting | bytes 12288 | tf_op jit(solution)/shard_map/reshape | solution.py:363
  51.6 0.6 %copy.19 = bf16[1,2,12,128]{3,1,2,0:T(2,128)(2,1)} copy(bf16[1,2,12,128]{3,2,1,0:T(8,128)(2,1)S(1)} %bitcast.12) | data formatting | bytes 12288

commit v3 on v2

--- a/solution.py
+++ b/solution.py
@@ -19,6 +19,7 @@
 EXT = COLS + HD
 FFD = 336
 FFP = 384
+WIDE = 2 * FFP
 PAGES = 24
 PAGE = 16
 KV = PAGES * PAGE
@@ -26,11 +27,10 @@
 SS_HI, SS_LO = FFD % HD, FFD % HD + 1
 
 CHUNKS = ((4, 5, 3, 6), (7, 2, 1, 0))
-STEPS = "F0 G0 F1 G1 A0 A1 D0 E0 D1 E1"
+STEPS = ("G0", "G1", "A0", "A1", "D0", "D1")
 NC = len(CHUNKS)
 BASE = [sum(len(c) for c in CHUNKS[:j]) for j in range(NC)]
-ROW = {m: 32 * BASE[j] + 16 * i for j, c in enumerate(CHUNKS) for i, m in enumerate(c)}
-HALF = {m: 16 * (BASE[j] + i) for j, c in enumerate(CHUNKS) for i, m in enumerate(c)}
+ROW = {m: 16 * (BASE[j] + i) for j, c in enumerate(CHUNKS) for i, m in enumerate(c)}
 FAR = (4, 5, 3, 6, 2, 7, 1)
 NEAR = FAR[::-1]
 
@@ -39,10 +39,10 @@
     res_hbm, q_hbm, k_hbm, v_hbm, gain_hbm, wg_hbm, wu_hbm, wd_hbm,
     pt_hbm, lens_hbm, ids_hbm, gates_hbm,
     out_ref,
-    pt, lens, ids, gates, res, q, kp, vp, gain, wgu, wd,
-    s24, blk, p1, f16, xall, pay, rsb, hid, csend, crecv, r1s, r1r, r2s, r2r,
-    ld_sem, p1_s, p1_r, p2_s, p2_r, fw_s, fw_r, rs_s, rs_r, ag_s, ag_r,
-    co_s, co_r, r1_s, r1_r, r2_sm, r2_rm,
+    pt, lens, ids, gates, res, q, kp, vp, gain, wgu, wt, wd,
+    s24, blk, p1, f16, xall, pay, rsb, hid, r1s, r1r, r2s, r2r,
+    ld_sem, p1_s, p1_r, p2_s, p2_r, rs_s, rs_r, ag_s, ag_r,
+    wx_s, wx_r, r1_s, r1_r, r2_sm, r2_rm,
 ):
     sec, grp, x = lax.axis_index("sec"), lax.axis_index("grp"), lax.axis_index("tp")
     y, z, c = sec * 4 + grp // 16, (grp // 2) % 8, grp % 2
@@ -120,9 +120,10 @@
             weight = jnp.where(hit, gates[s, k], weight)
     weight = weight / total
 
-    wd[FFD:, :] = jnp.zeros((FFP - FFD, COLS), BF16)
-    wgu[FFD:FFP, :] = jnp.zeros((FFP - FFD, COLS), BF16)
-    wgu[FFP + FFD :, :] = jnp.zeros((FFP - FFD, COLS), BF16)
+    for top in (FFD, FFP + FFD):
+        wd[top : top + FFP - FFD, :] = jnp.zeros((FFP - FFD, COLS), BF16)
+    for top in (FFD, FFP + FFD):
+        wgu[top : top + FFP - FFD, :] = jnp.zeros((FFP - FFD, COLS), BF16)
 
     def stack(value):
         for h in range(HEADS_DEV):
@@ -174,6 +175,21 @@
         send(blk, p1.at[k], p1_s.at[k], p1_r.at[k], first(k)) for k in range(1, RING)
     ]
 
+    for cp in loads[9:]:
+        cp.wait()
+    for part in range(2):
+        for t in range(0, FFP, HD):
+            left = part * WIDE + t
+            wt[:, left : left + HD] = wgu[part * FFP + t : part * FFP + t + HD, :].T
+    weights = [
+        send(src, dst, wx_s.at[i], wx_r.at[i], other)
+        for i, (src, dst) in enumerate((
+            (wt.at[:, pl.ds(0, FFP)], wt.at[:, pl.ds(FFP, FFP)]),
+            (wt.at[:, pl.ds(WIDE, FFP)], wt.at[:, pl.ds(WIDE + FFP, FFP)]),
+            (wd.at[pl.ds(0, FFD)], wd.at[pl.ds(FFP, FFD)]),
+        ))
+    ]
+
     def place(k, value):
         for t in range(EXT // HD):
             f16[2 * k : 2 * k + 2, t * HD : (t + 1) * HD] = value[2 * t : 2 * t + 2, :]
@@ -191,42 +207,30 @@
         )
         for m in FAR
     }
-    for cp in loads[9:]:
-        cp.wait()
-
-    forwards, rs, ag, core, back = {}, {}, {}, {}, {}
+
+    rs, ag, back = {}, {}, {}
 
     def quarter(j, q):
-        size = 8 * len(CHUNKS[j])
-        return pl.ds(pl.multiple_of(32 * BASE[j] + q * size, 16), size)
-
-    def forward(j):
-        n, base = len(CHUNKS[j]), 32 * BASE[j]
-        forwards[j] = []
-        for i, m in enumerate(CHUNKS[j]):
+        size = 4 * len(CHUNKS[j])
+        return pl.ds(pl.multiple_of(16 * BASE[j] + q * size, 16), size)
+
+    def gate_up(j):
+        n = len(CHUNKS[j])
+        for m in CHUNKS[j]:
             if m:
                 arrive2[m].wait_recv()
-            forwards[j].append(send(
-                xall.at[pl.ds(base + 16 * i, 16)],
-                xall.at[pl.ds(base + 16 * (n + i), 16)],
-                fw_s.at[m], fw_r.at[m], other,
-            ))
-
-    def gate_up(j):
-        n, base = len(CHUNKS[j]), 32 * BASE[j]
-        for cp in forwards[j]:
-            cp.wait_recv()
-        rows = pl.ds(base, 32 * n)
-        both = lax.dot_general(
-            xall[rows, 0:COLS], wgu[...], nt, preferred_element_type=F32
-        )
-        lane = lax.broadcasted_iota(jnp.int32, (32 * n, HD), 1)
+        if j == 0:
+            weights[0].wait_recv()
+            weights[1].wait_recv()
+        rows = pl.ds(16 * BASE[j], 16 * n)
+        both = jnp.dot(xall[rows, 0:COLS], wt[...], preferred_element_type=F32)
+        lane = lax.broadcasted_iota(jnp.int32, (16 * n, HD), 1)
         extras = xall[rows, COLS:EXT].astype(F32)
         tile = jnp.where(lane >= FFD % HD, extras, both[:, 256:FFP])
         pay[rows, 0:256] = both[:, 0:256].astype(BF16)
         pay[rows, 256:FFP] = tile.astype(BF16)
         pay[rows, FFP:] = both[:, FFP:].astype(BF16)
-        piece = pl.ds(8 * BASE[j], 8 * n)
+        piece = pl.ds(4 * BASE[j], 4 * n)
         rs[j] = [
             send(
                 pay.at[quarter(j, (x + e) % NX)], rsb.at[e, piece],
@@ -238,7 +242,7 @@
     def activate(j):
         n = len(CHUNKS[j])
         both = pay[quarter(j, x), :].astype(F32)
-        lane = lax.broadcasted_iota(jnp.int32, (8 * n, HD), 1)
+        lane = lax.broadcasted_iota(jnp.int32, (4 * n, HD), 1)
         weight = jnp.sum(
             jnp.where(
                 (lane == y) | (lane == y + 8),
@@ -248,16 +252,16 @@
         )
         for cp, e in zip(rs[j], (2, 1, 3)):
             cp.wait_recv()
-            both = both + rsb[e, pl.ds(8 * BASE[j], 8 * n), :].astype(F32)
+            both = both + rsb[e, pl.ds(4 * BASE[j], 4 * n), :].astype(F32)
         square = jnp.sum(
             jnp.where((lane == SS_HI) | (lane == SS_LO), both[:, 256:FFP], 0.0),
             axis=1, keepdims=True,
         )
         scale = lax.rsqrt(square / D + 1e-05)
-        gate = both[:, 0:FFP] * scale
-        up = both[:, FFP:] * (scale * weight)
+        gate = both[:, 0:WIDE] * scale
+        up = both[:, WIDE:] * (scale * weight)
         value = gate / (1.0 + jnp.exp(-gate)) * up
-        unit = lax.broadcasted_iota(jnp.int32, (8 * n, FFP), 1)
+        unit = lax.broadcasted_iota(jnp.int32, (4 * n, WIDE), 1) % FFP
         mine = quarter(j, x)
         hid[mine, :] = jnp.where(unit < FFD, value, 0.0).astype(BF16)
         ag[j] = [
@@ -266,36 +270,27 @@
         ]
 
     def down(j):
-        n, base = len(CHUNKS[j]), 32 * BASE[j]
-        half = pl.ds(16 * BASE[j], 16 * n)
+        n = len(CHUNKS[j])
+        if j == 0:
+            weights[2].wait_recv()
         for cp in ag[j]:
             cp.wait_recv()
-        theirs = pl.ds(base + 16 * n, 16 * n)
-        csend[half, :] = jnp.dot(
-            hid[theirs, :], wd[...], preferred_element_type=F32
+        half = pl.ds(16 * BASE[j], 16 * n)
+        r1s[half, :] = jnp.dot(
+            hid[half, :], wd[...], preferred_element_type=F32
         ).astype(BF16)
-        core[j] = send(csend.at[half], crecv.at[half], co_s.at[j], co_r.at[j], other)
-        mine = pl.ds(base, 16 * n)
-        r1s[half, :] = jnp.dot(
-            hid[mine, :], wd[...], preferred_element_type=F32
-        ).astype(BF16)
-
-    def give_back(j):
-        core[j].wait_recv()
-        half = pl.ds(16 * BASE[j], 16 * len(CHUNKS[j]))
-        r1s[half, :] = (r1s[half, :].astype(F32) + crecv[half, :].astype(F32)).astype(BF16)
         for m in FAR:
             if m in CHUNKS[j]:
                 back[m] = send(
-                    r1s.at[pl.ds(HALF[m], 16)], r1r.at[m],
+                    r1s.at[pl.ds(ROW[m], 16)], r1r.at[m],
                     r1_s.at[m], r1_r.at[m], second(RING - m),
                 )
 
-    stages = {"F": forward, "G": gate_up, "A": activate, "D": down, "E": give_back}
-    for step in STEPS.split():
+    stages = {"G": gate_up, "A": activate, "D": down}
+    for step in STEPS:
         stages[step[0]](int(step[1:]))
 
-    total = r1s[pl.ds(HALF[0], 16), :].astype(F32)
+    total = r1s[pl.ds(ROW[0], 16), :].astype(F32)
     for m in NEAR:
         back[m].wait_recv()
         total = total + r1r[m].astype(F32)
@@ -339,18 +334,18 @@
             pltpu.VMEM((2, COLS), BF16), pltpu.VMEM((2, COLS), BF16),
             pltpu.VMEM((PAGES, PAGE, 2 * HD), BF16), pltpu.VMEM((PAGES, PAGE, 2 * HD), BF16),
             pltpu.VMEM((COLS,), BF16),
-            pltpu.VMEM((2 * FFP, COLS), BF16),
-            pltpu.VMEM((FFP, COLS), BF16),
+            pltpu.VMEM((WIDE, COLS), BF16), pltpu.VMEM((COLS, 2 * WIDE), BF16),
+            pltpu.VMEM((WIDE, COLS), BF16),
             pltpu.VMEM((24, HD), F32), pltpu.VMEM((BLK, HD), BF16),
             pltpu.VMEM((RING, BLK, HD), BF16), pltpu.VMEM((16, EXT), F32),
-            pltpu.VMEM((256, EXT), BF16), pltpu.VMEM((256, 2 * FFP), BF16),
-            pltpu.VMEM((NX, 64, 2 * FFP), BF16), pltpu.VMEM((256, FFP), BF16),
-            pltpu.VMEM((128, COLS), BF16), pltpu.VMEM((128, COLS), BF16),
+            pltpu.VMEM((128, EXT), BF16), pltpu.VMEM((128, 2 * WIDE), BF16),
+            pltpu.VMEM((NX, 32, 2 * WIDE), BF16),
+            pltpu.VMEM((128, WIDE), BF16),
             pltpu.VMEM((128, COLS), BF16), pltpu.VMEM((RING, 16, COLS), BF16),
             pltpu.VMEM((RING, BLK, HD), BF16), pltpu.VMEM((RING, BLK, HD), BF16),
             dma((12,)), dma((RING,)), dma((RING,)), dma((RING,)), dma((RING,)),
-            dma((RING,)), dma((RING,)), dma((NC, NX)), dma((NC, NX)), dma((NC, NX)), dma((NC, NX)),
-            dma((NC,)), dma((NC,)), dma((RING,)), dma((RING,)), dma((RING,)), dma((RING,)),
+            dma((NC, NX)), dma((NC, NX)), dma((NC, NX)), dma((NC, NX)),
+            dma((3,)), dma((3,)), dma((RING,)), dma((RING,)), dma((RING,)), dma((RING,)),
         ],
         compiler_params=pltpu.CompilerParams(
             collective_id=0, has_side_effects=True, vmem_limit_bytes=60 * 2**20

time: 52.4 us -> 50.5 us (0.964)
  the two profiles are of different devices: /device:TPU:1 before, /device:TPU:8 now
where the time goes in v3:
time: 50.5 us; the launch traced here: 50.3 us
  Pallas kernels  49 us (97%)
  local copies, waits for them, and re-layouts  1.3 us (3%)
    pallas_call x1, Pallas kernels, shards(): pl.pallas_call(kernel, out_shape=jax.ShapeDtypeStruct((24, HD), BF16), in...  49 us

profile of v3, /device:TPU:8, one launch (start us, length us, event | category | flops | bytes accessed | tf_op | source)
XLA Modules:
  0.0 50.3 jit_solution(18008006858870320714)
XLA Ops:
  0.0 49.0 %decode_layer.1 = bf16[24,128]{1,0:T(8,128)(2,1)} custom-call(bf16[2,1536]{1,0:T(2,128)(2,1)} %res_hbm.1, bf16[2,1536]{1,0:T(2,128)(2,1)} %q_hbm.1, bf16[24,16,256]{2,1,0:T(8,128)(2,1)} %k_hbm.1, bf16[24,16,256]{2,1,0:T(8,128)(2,1)} %v_hbm.1, bf16[1536]{0:T(1024)(128)(2,1)} %gain_hbm.1, bf16[336,1536]{1,0:T(8,128)(2,1)} %bitcast.10, ...), custom_call_target="tpu_custom_call" | custom-call | tf_op jit(solution)/shard_map/decode_layer/pallas_call | solution.py:326
  49.0 0.7 %copy.18 = bf16[12,2,128]{2,0,1:T(8,128)(2,1)S(1)} copy(bf16[12,2,128]{2,1,0:T(2,128)(2,1)} %bitcast.13) | data formatting | bytes 12288 | tf_op jit(solution)/shard_map/reshape | solution.py:358
  49.7 0.6 %copy.19 = bf16[1,2,12,128]{3,1,2,0:T(2,128)(2,1)} copy(bf16[1,2,12,128]{3,2,1,0:T(8,128)(2,1)S(1)} %bitcast.12) | data formatting | bytes 12288

commit v4 on v3

--- a/solution.py
+++ b/solution.py
@@ -68,16 +68,17 @@
         pl.semaphore_signal(barrier, inc=1, device_id=peer, device_id_type=MESH)
 
     loads = []
-    for i, (a, b) in enumerate((
+
+    def load(*pairs):
+        for src, dst in pairs:
+            cp = pltpu.make_async_copy(src, dst, ld_sem.at[len(loads)])
+            cp.start()
+            loads.append(cp)
+
+    load(
         (pt_hbm, pt), (lens_hbm, lens), (ids_hbm, ids), (gates_hbm, gates),
         (q_hbm, q), (k_hbm, kp), (v_hbm, vp), (res_hbm, res), (gain_hbm, gain),
-        (wg_hbm, wgu.at[pl.ds(0, FFD)]), (wu_hbm, wgu.at[pl.ds(FFP, FFD)]),
-        (wd_hbm, wd.at[pl.ds(0, FFD)]),
-    )):
-        cp = pltpu.make_async_copy(a, b, ld_sem.at[i])
-        cp.start()
-        loads.append(cp)
-
+    )
     pending = []
 
     def send(src, dst, ssem, rsem, to):
@@ -170,9 +171,13 @@
     blk[...] = jnp.concatenate([stream * gain24, extra], axis=0).astype(BF16)
 
     pl.semaphore_wait(barrier, len(peers))
+    load(
+        (wg_hbm, wgu.at[pl.ds(0, FFD)]), (wu_hbm, wgu.at[pl.ds(FFP, FFD)]),
+        (wd_hbm, wd.at[pl.ds(0, FFD)]),
+    )
 
     arrive1 = [
-        send(blk, p1.at[k], p1_s.at[k], p1_r.at[k], first(k)) for k in range(1, RING)
+        send(blk, p1.at[k], p1_s.at[k], p1_r.at[k], first(k)) for k in FAR
     ]
 
     for cp in loads[9:]:
@@ -196,7 +201,7 @@
 
     place(0, blk[...].astype(F32))
     for k in NEAR:
-        arrive1[k - 1].wait_recv()
+        arrive1[FAR.index(k)].wait_recv()
         place(k, p1[k].astype(F32))
     own = pl.ds(ROW[0], 16)
     xall[own, :] = f16[...].astype(BF16)
@@ -223,21 +228,22 @@
             weights[0].wait_recv()
             weights[1].wait_recv()
         rows = pl.ds(16 * BASE[j], 16 * n)
-        both = jnp.dot(xall[rows, 0:COLS], wt[...], preferred_element_type=F32)
         lane = lax.broadcasted_iota(jnp.int32, (16 * n, HD), 1)
         extras = xall[rows, COLS:EXT].astype(F32)
-        tile = jnp.where(lane >= FFD % HD, extras, both[:, 256:FFP])
-        pay[rows, 0:256] = both[:, 0:256].astype(BF16)
-        pay[rows, 256:FFP] = tile.astype(BF16)
-        pay[rows, FFP:] = both[:, FFP:].astype(BF16)
         piece = pl.ds(4 * BASE[j], 4 * n)
-        rs[j] = [
-            send(
-                pay.at[quarter(j, (x + e) % NX)], rsb.at[e, piece],
-                rs_s.at[j, e], rs_r.at[j, e], along(e),
-            )
-            for e in (2, 1, 3)
-        ]
+        rs[j] = {}
+        for h in range(2):
+            cols = pl.ds(h * WIDE, WIDE)
+            half = jnp.dot(xall[rows, 0:COLS], wt[:, cols], preferred_element_type=F32)
+            pay[rows, cols] = half.astype(BF16)
+            if h == 0:
+                tile = jnp.where(lane >= FFD % HD, extras, half[:, 256:FFP])
+                pay[rows, 256:FFP] = tile.astype(BF16)
+            for e in (2, 1, 3):
+                rs[j][e, h] = send(
+                    pay.at[quarter(j, (x + e) % NX), cols], rsb.at[e, piece, cols],
+                    rs_s.at[j, e, h], rs_r.at[j, e, h], along(e),
+                )
 
     def activate(j):
         n = len(CHUNKS[j])
@@ -250,8 +256,9 @@
             ),
             axis=1, keepdims=True,
         )
-        for cp, e in zip(rs[j], (2, 1, 3)):
-            cp.wait_recv()
+        for e in (2, 1, 3):
+            rs[j][e, 0].wait_recv()
+            rs[j][e, 1].wait_recv()
             both = both + rsb[e, pl.ds(4 * BASE[j], 4 * n), :].astype(F32)
         square = jnp.sum(
             jnp.where((lane == SS_HI) | (lane == SS_LO), both[:, 256:FFP], 0.0),
@@ -344,7 +351,7 @@
             pltpu.VMEM((128, COLS), BF16), pltpu.VMEM((RING, 16, COLS), BF16),
             pltpu.VMEM((RING, BLK, HD), BF16), pltpu.VMEM((RING, BLK, HD), BF16),
             dma((12,)), dma((RING,)), dma((RING,)), dma((RING,)), dma((RING,)),
-            dma((NC, NX)), dma((NC, NX)), dma((NC, NX)), dma((NC, NX)),
+            dma((NC, NX, 2)), dma((NC, NX, 2)), dma((NC, NX)), dma((NC, NX)),
             dma((3,)), dma((3,)), dma((RING,)), dma((RING,)), dma((RING,)), dma((RING,)),
         ],
         compiler_params=pltpu.CompilerParams(

time: 50.5 us -> 50.2 us (level)
  no operation moved by 1% of the time
where the time goes in v4:
time: 50.2 us; the launch traced here: 50 us
  Pallas kernels  48.7 us (97%)
  local copies, waits for them, and re-layouts  1.3 us (3%)
    pallas_call x1, Pallas kernels, shards(): pl.pallas_call(kernel, out_shape=jax.ShapeDtypeStruct((24, HD), BF16), in...  48.7 us

profile of v4, /device:TPU:8, one launch (start us, length us, event | category | flops | bytes accessed | tf_op | source)
XLA Modules:
  0.0 50.0 jit_solution(2231356329860968306)
XLA Ops:
  0.0 48.7 %decode_layer.1 = bf16[24,128]{1,0:T(8,128)(2,1)} custom-call(bf16[2,1536]{1,0:T(2,128)(2,1)} %res_hbm.1, bf16[2,1536]{1,0:T(2,128)(2,1)} %q_hbm.1, bf16[24,16,256]{2,1,0:T(8,128)(2,1)} %k_hbm.1, bf16[24,16,256]{2,1,0:T(8,128)(2,1)} %v_hbm.1, bf16[1536]{0:T(1024)(128)(2,1)} %gain_hbm.1, bf16[336,1536]{1,0:T(8,128)(2,1)} %bitcast.10, ...), custom_call_target="tpu_custom_call" | custom-call | tf_op jit(solution)/shard_map/decode_layer/pallas_call | solution.py:333
  48.7 0.7 %copy.18 = bf16[12,2,128]{2,0,1:T(8,128)(2,1)S(1)} copy(bf16[12,2,128]{2,1,0:T(2,128)(2,1)} %bitcast.13) | data formatting | bytes 12288 | tf_op jit(solution)/shard_map/reshape | solution.py:365
  49.4 0.6 %copy.19 = bf16[1,2,12,128]{3,1,2,0:T(2,128)(2,1)} copy(bf16[1,2,12,128]{3,2,1,0:T(8,128)(2,1)S(1)} %bitcast.12) | data formatting | bytes 12288

commit v5 on v4

--- a/solution.py
+++ b/solution.py
@@ -208,7 +208,16 @@
 
     arrive2 = {
         m: send(
-            xall.at[own], xall.at[pl.ds(ROW[m], 16)], p2_s.at[m], p2_r.at[m], second(m)
+            xall.at[own, pl.ds(0, COLS)], xall.at[pl.ds(ROW[m], 16), pl.ds(0, COLS)],
+            p2_s.at[m, 0], p2_r.at[m, 0], second(m),
+        )
+        for m in FAR
+    }
+    last = pl.ds(COLS, HD)
+    tails = {
+        m: send(
+            xall.at[own, last], xall.at[pl.ds(ROW[m], 16), last],
+            p2_s.at[m, 1], p2_r.at[m, 1], second(m),
         )
         for m in FAR
     }
@@ -229,7 +238,6 @@
             weights[1].wait_recv()
         rows = pl.ds(16 * BASE[j], 16 * n)
         lane = lax.broadcasted_iota(jnp.int32, (16 * n, HD), 1)
-        extras = xall[rows, COLS:EXT].astype(F32)
         piece = pl.ds(4 * BASE[j], 4 * n)
         rs[j] = {}
         for h in range(2):
@@ -237,6 +245,10 @@
             half = jnp.dot(xall[rows, 0:COLS], wt[:, cols], preferred_element_type=F32)
             pay[rows, cols] = half.astype(BF16)
             if h == 0:
+                for m in CHUNKS[j]:
+                    if m:
+                        tails[m].wait_recv()
+                extras = xall[rows, COLS:EXT].astype(F32)
                 tile = jnp.where(lane >= FFD % HD, extras, half[:, 256:FFP])
                 pay[rows, 256:FFP] = tile.astype(BF16)
             for e in (2, 1, 3):
@@ -350,7 +362,7 @@
             pltpu.VMEM((128, WIDE), BF16),
             pltpu.VMEM((128, COLS), BF16), pltpu.VMEM((RING, 16, COLS), BF16),
             pltpu.VMEM((RING, BLK, HD), BF16), pltpu.VMEM((RING, BLK, HD), BF16),
-            dma((12,)), dma((RING,)), dma((RING,)), dma((RING,)), dma((RING,)),
+            dma((12,)), dma((RING,)), dma((RING,)), dma((RING, 2)), dma((RING, 2)),
             dma((NC, NX, 2)), dma((NC, NX, 2)), dma((NC, NX)), dma((NC, NX)),
             dma((3,)), dma((3,)), dma((RING,)), dma((RING,)), dma((RING,)), dma((RING,)),
         ],

time: 50.2 us -> 51.9 us (1.034)
  Pallas kernels: 48.7 us -> 50.4 us
    pallas_call x1, Pallas kernels: 48.7 us -> 50.4 us  [shards(): pl.pallas_call(kernel, out_shape=jax.ShapeDtypeStruct((24, HD), BF16), in...]
where the time goes in v5:
time: 51.9 us; the launch traced here: 51.7 us
  Pallas kernels  50.4 us (97%)
  local copies, waits for them, and re-layouts  1.3 us (3%)
    pallas_call x1, Pallas kernels, shards(): pl.pallas_call(kernel, out_shape=jax.ShapeDtypeStruct((24, HD), BF16), in...  50.4 us

profile of v5, /device:TPU:8, one launch (start us, length us, event | category | flops | bytes accessed | tf_op | source)
XLA Modules:
  0.0 51.7 jit_solution(11096177081402693105)
XLA Ops:
  0.0 50.4 %decode_layer.1 = bf16[24,128]{1,0:T(8,128)(2,1)} custom-call(bf16[2,1536]{1,0:T(2,128)(2,1)} %res_hbm.1, bf16[2,1536]{1,0:T(2,128)(2,1)} %q_hbm.1, bf16[24,16,256]{2,1,0:T(8,128)(2,1)} %k_hbm.1, bf16[24,16,256]{2,1,0:T(8,128)(2,1)} %v_hbm.1, bf16[1536]{0:T(1024)(128)(2,1)} %gain_hbm.1, bf16[336,1536]{1,0:T(8,128)(2,1)} %bitcast.10, ...), custom_call_target="tpu_custom_call" | custom-call | tf_op jit(solution)/shard_map/decode_layer/pallas_call | solution.py:345
  50.4 0.7 %copy.18 = bf16[12,2,128]{2,0,1:T(8,128)(2,1)S(1)} copy(bf16[12,2,128]{2,1,0:T(2,128)(2,1)} %bitcast.13) | data formatting | bytes 12288 | tf_op jit(solution)/shard_map/reshape | solution.py:377
  51.1 0.6 %copy.19 = bf16[1,2,12,128]{3,1,2,0:T(2,128)(2,1)} copy(bf16[1,2,12,128]{3,2,1,0:T(8,128)(2,1)S(1)} %bitcast.12) | data formatting | bytes 12288
